TPU v7x, 512 devices: a whole 4x4x16 slice. The times are simulated.
512 devices in a mesh: expert: 64 (over z, y), context: 4 (over x), pipe: 2 (over core).
Axes of the slice: x: 4, y: 4, z: 16, core: 2. Of those that a mesh axis runs over, the one named last changes fastest.
Arguments:
- hidden_in: bfloat16 [448, 3584], P('expert'), may hold values from -6 to 6
- draft_embeds: bfloat16 [2, 448, 3584], P(None, 'expert'), may hold values from -6 to 6
- norm_gains: float32 [2, 3584], replicated, may hold values from 0.1 to 1.9
- queries: bfloat16 [2, 448, 64, 576], P(None, 'expert'), may hold values from -72 to 72
- latent_cache: bfloat16 [448, 1024, 576], P('expert', ('context', 'pipe')), may hold values from -6 to 6
- lengths: int32 [448], P('expert'), may hold values from 2 to 1024, as said below
- route_ids: int32 [2, 448, 8], P(None, 'expert'), may hold values from 0 to 63, all different within a row; in each aligned block of 7 rows (0 to 6, 7 to 13, ..., all dimensions but the last counted through in order) at most 2 rows name the same one
- route_weights: float32 [2, 448, 8], P(None, 'expert'), may hold values from 0.1 to 0.6
- w_gate: bfloat16 [64, 3584, 1024], P('expert', None, ('context', 'pipe')), may hold values from -0.09375 to 0.09375
- w_up: bfloat16 [64, 3584, 1024], P('expert', None, ('context', 'pipe')), may hold values from -0.09375 to 0.09375
- w_down: bfloat16 [64, 1024, 3584], P('expert', ('context', 'pipe')), may hold values from -0.1875 to 0.1875
Outputs:
- attended: bfloat16 [2, 448, 64, 512], P(None, 'expert', ('context', 'pipe'))
- hidden_out: bfloat16 [448, 3584], P('expert')
Inputs may be any that keep to these rules, and one draw needn't show every extreme that they name: `route_ids`: each row names 8 different experts. Among the 7 rows of one index of expert in one step, no expert is named by more than 2 rows, a bound that some block reaches. `lengths`: some row has all 1024 positions live in every draw.
All inputs are finite; a program needn't handle non-finite values.
Results may differ from a plain program's by a relative error of at most 0.024.
Values may be sent and summed in bfloat16 or wider, within the bound.
A program may use at most 128 MiB of HBM per device.

v0:
```python
import jax
import jax.numpy as jnp
from jax import lax
from jax.sharding import PartitionSpec as P

LATENT = 512
EXPERTS = 64
TOPK = 8
CAP = 2
LOOPS = 2


EPSILON = 1e-06
NEG_FILL = -1e30


def normalize(values, gain):
    values = values.astype(jnp.float32)
    return values * lax.rsqrt(jnp.mean(values * values, axis=-1, keepdims=True) + EPSILON) * gain


def body(
    hidden_in,
    draft_embeds,
    norm_gains,
    queries,
    latent_cache,
    lengths,
    route_ids,
    route_weights,
    w_gate,
    w_up,
    w_down,
):
    group_index = lax.axis_index(("context", "pipe"))
    local_rows = hidden_in.shape[0]
    model_width = hidden_in.shape[1]
    local_ctx = latent_cache.shape[1]
    scale_factor = float(queries.shape[3]) ** (-0.5)
    positions = group_index * local_ctx + jnp.arange(local_ctx, dtype=jnp.int32)
    visible = positions[None, :] < lengths[:, None]
    cache_values = latent_cache[:, :, :LATENT]
    expert_ids = jnp.arange(EXPERTS, dtype=jnp.int32)
    hidden = hidden_in
    results = []
    for loop_index in range(LOOPS):
        scores = (
            jnp.einsum(
                "rhc,rtc->rht",
                queries[loop_index],
                latent_cache,
                preferred_element_type=jnp.float32,
            )
            * scale_factor
        )
        scores = jnp.where(visible[:, None, :], scores, NEG_FILL)
        largest = jnp.max(scores, axis=-1)
        weights = jnp.where(visible[:, None, :], jnp.exp(scores - largest[..., None]), 0.0).astype(
            jnp.bfloat16
        )
        total = jnp.sum(weights.astype(jnp.float32), axis=-1)
        summed = jnp.einsum(
            "rht,rtl->rhl", weights, cache_values, preferred_element_type=jnp.float32
        )
        tops, totals, sums = (
            lax.all_to_all(
                largest[None].astype(jnp.bfloat16),
                ("context", "pipe"),
                split_axis=2,
                concat_axis=0,
                tiled=True,
            ).astype(jnp.float32),
            lax.all_to_all(
                total[None].astype(jnp.bfloat16),
                ("context", "pipe"),
                split_axis=2,
                concat_axis=0,
                tiled=True,
            ).astype(jnp.float32),
            lax.all_to_all(
                summed[None].astype(jnp.bfloat16),
                ("context", "pipe"),
                split_axis=2,
                concat_axis=0,
                tiled=True,
            ).astype(jnp.float32),
        )
        top_all = jnp.max(tops, axis=0)
        factors = jnp.exp(tops - top_all[None])
        total_all = jnp.sum(totals * factors, axis=0)
        summed_all = jnp.sum(sums * factors[..., None], axis=0)
        results.append((summed_all / total_all[..., None]).astype(jnp.bfloat16))
        mixed = normalize(hidden, norm_gains[0]) + normalize(
            draft_embeds[loop_index], norm_gains[1]
        )
        mixed_low = mixed.astype(jnp.bfloat16)
        chosen_ids = route_ids[loop_index]
        onehot = (chosen_ids[:, :, None] == expert_ids[None, None, :]).astype(jnp.int32)
        chosen = jnp.sum(onehot, axis=1)
        earlier = jnp.cumsum(chosen, axis=0) - chosen
        slot_index = jnp.take_along_axis(earlier, chosen_ids, axis=1)
        buffer = jnp.zeros((EXPERTS, CAP, model_width), jnp.bfloat16)
        buffer = buffer.at[chosen_ids, slot_index].set(
            jnp.broadcast_to(mixed_low[:, None, :], (local_rows, TOPK, model_width))
        )
        received = lax.all_to_all(buffer, "expert", split_axis=0, concat_axis=1, tiled=True)
        gate_out = jnp.einsum("emd,edf->emf", received, w_gate, preferred_element_type=jnp.float32)
        up_out = jnp.einsum("emd,edf->emf", received, w_up, preferred_element_type=jnp.float32)
        active = (jax.nn.silu(gate_out) * up_out).astype(jnp.bfloat16)
        partial_out = jnp.einsum("emf,efd->emd", active, w_down, preferred_element_type=jnp.float32)
        gate_scale = route_weights[loop_index][:, :, None]
        expert_sums = lax.psum_scatter(
            partial_out.astype(jnp.bfloat16), ("context", "pipe"), scatter_dimension=2, tiled=True
        ).astype(jnp.float32)
        returned = lax.all_to_all(
            expert_sums.astype(jnp.bfloat16), "expert", split_axis=1, concat_axis=0, tiled=True
        ).astype(expert_sums.dtype)
        picked = returned[chosen_ids, slot_index]
        routed_part = jnp.sum(gate_scale * picked, axis=1)
        routed = lax.all_gather(routed_part, ("context", "pipe"), axis=1, tiled=True)
        hidden = (mixed + routed).astype(jnp.bfloat16)
    return (jnp.stack(results), hidden)


def solution(mesh):
    in_specs = (
        P("expert", None),
        P(None, "expert", None),
        P(),
        P(None, "expert", None, None),
        P("expert", ("context", "pipe"), None),
        P("expert"),
        P(None, "expert", None),
        P(None, "expert", None),
        P("expert", None, ("context", "pipe")),
        P("expert", None, ("context", "pipe")),
        P("expert", ("context", "pipe"), None),
    )
    out_specs = (P(None, "expert", ("context", "pipe"), None), P("expert", None))
    return jax.shard_map(body, mesh=mesh, in_specs=in_specs, out_specs=out_specs, check_vma=False)
```

profile of v0, /device:TPU:1, one launch (start us, length us, event | category | flops | bytes accessed | tf_op | source)
XLA Modules:
  0.0 378.5 jit_solution(15908700571363661608)
XLA Ops:
  12.4 8.9 %scatter_fusion = bf16[64,2,3584]{2,1,0:T(2,128)(2,1)S(1)} fusion(bf16[64,2,3584]{2,1,0:T(2,128)(2,1)S(1)} %broadcast.154.clone, s32[56]{0:T(128)S(1)} %reshape.349, bf16[56,3584]{1,0:T(8,128)(2,1)S(1)} %broadcast_bitcast_fusion.1), kind=kCustom, calls=%fused_computation.4 | custom fusion | bytes 1204672 | tf_op jit(solution)/shard_map/scatter | solution.py:103
  21.3 65.2 %all_to_all.102 = bf16[64,2,3584]{2,1,0:T(2,128)(2,1)S(1)} all-to-all(bf16[64,2,3584]{2,1,0:T(2,128)(2,1)S(1)} %scatter_fusion), channel_id=1, replica_groups=mesh['expert'=64,'context'=4,'pipe'=2] {'expert'}, dimensions={0} | all-to-all | bytes 1835008 | tf_op jit(solution)/shard_map/all_to_all | solution.py:106
  86.8 1.6 fusion.18
  88.5 1.7 fusion
  90.2 4.3 %copy.216 = bf16[1,128,3584]{1,0,2:T(2,128)(2,1)S(1)} copy(bf16[1,128,3584]{2,1,0:T(8,128)(2,1)} %fusion) | data formatting | bytes 1835008
  95.5 33.2 %reduce-scatter.7.cloned.1.call-done = bf16[448,128]{1,0:T(8,128)(2,1)} async-done(((bf16[3584,128]{1,0:T(8,128)(2,1)}), bf16[448,128]{1,0:T(8,128)(2,1)}) %reduce-scatter.7.cloned.1.call-update) | async-done | bytes 114704
  131.0 1.5 reduce.26
  133.2 14.4 %all-to-all-start.7 = ((bf16[64,2,448]{2,1,0:T(2,128)(2,1)}), bf16[64,2,448]{2,1,0:T(2,128)(2,1)S(1)}, u32[]{:S(2)}, u32[]{:S(2)}) async-start(bf16[64,2,448]{2,1,0:T(2,128)(2,1)} %reshape.401), calls=%async_computation.7 | async-start | bytes 262144 | tf_op jit(solution)/shard_map/all_to_all | solution.py:115
  148.4 14.2 %all-to-all-done.7 = bf16[64,2,448]{2,1,0:T(2,128)(2,1)S(1)} async-done(((bf16[64,2,448]{2,1,0:T(2,128)(2,1)}), bf16[64,2,448]{2,1,0:T(2,128)(2,1)S(1)}, u32[]{:S(2)}, u32[]{:S(2)}) %all-to-all-start.7) | async-done | bytes 114720 | tf_op jit(solution)/shard_map/all_to_all | solution.py:115
  164.7 17.5 %all-gather = f32[8,448,7]{1,2,0:T(8,128)S(1)} all-gather(f32[1,448,7]{1,2,0:T(8,128)S(1)} %bitcast.217), channel_id=1, replica_groups=mesh['expert'=64,'context'=4,'pipe'=2] {'context','pipe'}, dimensions={0}, use_global_device_ids=true | all-gather | bytes 112896 | tf_op jit(solution)/shard_map/all_gather | solution.py:120
  184.8 14.3 %scatter_fusion.1 = bf16[64,2,3584]{2,1,0:T(2,128)(2,1)} fusion(bf16[64,2,3584]{2,1,0:T(2,128)(2,1)} %broadcast.154, s32[56]{0:T(128)S(1)} %reshape.355, bf16[56,3584]{1,0:T(8,128)(2,1)S(1)} %broadcast_bitcast_fusion), kind=kCustom, calls=%fused_computation.5 | custom fusion | bytes 1204672 | tf_op jit(solution)/shard_map/scatter | solution.py:103
  199.2 4.8 %all-to-all-start.8 = ((bf16[64,2,3584]{2,1,0:T(2,128)(2,1)}), bf16[64,2,3584]{2,1,0:T(2,128)(2,1)S(1)}, u32[]{:S(2)}, u32[]{:S(2)}) async-start(bf16[64,2,3584]{2,1,0:T(2,128)(2,1)} %scatter_fusion.1), calls=%async_computation.8 | async-start | bytes 1835008 | tf_op jit(solution)/shard_map/all_to_all | solution.py:106
  208.6 43.6 %all-to-all-done.8 = bf16[64,2,3584]{2,1,0:T(2,128)(2,1)S(1)} async-done(((bf16[64,2,3584]{2,1,0:T(2,128)(2,1)}), bf16[64,2,3584]{2,1,0:T(2,128)(2,1)S(1)}, u32[]{:S(2)}, u32[]{:S(2)}) %all-to-all-start.8) | async-done | bytes 917536 | tf_op jit(solution)/shard_map/all_to_all | solution.py:106
  252.2 6.2 %all-to-all-start.1 = ((bf16[1,7,64]{1,0,2:T(2,128)(2,1)}), bf16[1,7,64]{1,0,2:T(2,128)(2,1)}, u32[]{:S(2)}, u32[]{:S(2)}) async-start(bf16[1,7,64]{1,0,2:T(2,128)(2,1)} %copy.188), calls=%async_computation.1 | async-start | bytes 65536 | tf_op jit(solution)/shard_map/all_to_all | solution.py:66
  258.4 2.5 reshape.309
  260.9 2.2 fusion.16
  263.1 2.8 fusion.1
  265.9 4.9 %copy.218 = bf16[1,128,3584]{1,0,2:T(2,128)(2,1)} copy(bf16[1,128,3584]{2,1,0:T(8,128)(2,1)} %fusion.1) | data formatting | bytes 1835008
  270.9 2.5 copy.266
  276.1 4.8 %all-to-all-start.2 = ((bf16[1,7,64]{1,0,2:T(2,128)(2,1)}), bf16[1,7,64]{1,0,2:T(2,128)(2,1)S(1)}, u32[]{:S(2)}, u32[]{:S(2)}) async-start(bf16[1,7,64]{1,0,2:T(2,128)(2,1)} %copy.191), calls=%async_computation.2 | async-start | bytes 65536 | tf_op jit(solution)/shard_map/all_to_all | solution.py:73
  286.0 4.8 %all-to-all-start.5 = ((bf16[1,7,64]{1,0,2:T(2,128)(2,1)}), bf16[1,7,64]{1,0,2:T(2,128)(2,1)S(1)}, u32[]{:S(2)}, u32[]{:S(2)}) async-start(bf16[1,7,64]{1,0,2:T(2,128)(2,1)} %copy.198), calls=%async_computation.5 | async-start | bytes 65536 | tf_op jit(solution)/shard_map/all_to_all | solution.py:73
  290.9 4.7 %all-to-all-done.5 = bf16[1,7,64]{1,0,2:T(2,128)(2,1)S(1)} async-done(((bf16[1,7,64]{1,0,2:T(2,128)(2,1)}), bf16[1,7,64]{1,0,2:T(2,128)(2,1)S(1)}, u32[]{:S(2)}, u32[]{:S(2)}) %all-to-all-start.5) | async-done | bytes 928 | tf_op jit(solution)/shard_map/all_to_all | solution.py:73
  295.6 4.0 %all-to-all-start.4 = ((bf16[1,7,64]{1,0,2:T(2,128)(2,1)}), bf16[1,7,64]{1,0,2:T(2,128)(2,1)S(1)}, u32[]{:S(2)}, u32[]{:S(2)}) async-start(bf16[1,7,64]{1,0,2:T(2,128)(2,1)} %copy.195), calls=%async_computation.4 | async-start | bytes 65536 | tf_op jit(solution)/shard_map/all_to_all | solution.py:66
  299.7 4.6 %all-to-all-done.4 = bf16[1,7,64]{1,0,2:T(2,128)(2,1)S(1)} async-done(((bf16[1,7,64]{1,0,2:T(2,128)(2,1)}), bf16[1,7,64]{1,0,2:T(2,128)(2,1)S(1)}, u32[]{:S(2)}, u32[]{:S(2)}) %all-to-all-start.4) | async-done | bytes 928 | tf_op jit(solution)/shard_map/all_to_all | solution.py:66
  304.4 4.1 %all-to-all-start = ((bf16[1,7,64,512]{3,1,0,2:T(8,128)(2,1)}), bf16[1,7,64,512]{3,1,0,2:T(8,128)(2,1)S(1)}, u32[]{:S(2)}, u32[]{:S(2)}) async-start(bf16[1,7,64,512]{3,1,0,2:T(8,128)(2,1)} %copy.187), calls=%async_computation | async-start | bytes 1048576 | tf_op jit(solution)/shard_map/all_to_all | solution.py:80
  309.1 8.9 %all-to-all-done = bf16[1,7,64,512]{3,1,0,2:T(8,128)(2,1)S(1)} async-done(((bf16[1,7,64,512]{3,1,0,2:T(8,128)(2,1)}), bf16[1,7,64,512]{3,1,0,2:T(8,128)(2,1)S(1)}, u32[]{:S(2)}, u32[]{:S(2)}) %all-to-all-start) | async-done | bytes 458784 | tf_op jit(solution)/shard_map/all_to_all | solution.py:80
  318.0 4.3 %all-to-all-start.3 = ((bf16[1,7,64,512]{3,1,0,2:T(8,128)(2,1)}), bf16[1,7,64,512]{3,1,0,2:T(8,128)(2,1)S(1)}, u32[]{:S(2)}, u32[]{:S(2)}) async-start(bf16[1,7,64,512]{3,1,0,2:T(8,128)(2,1)} %copy.194), calls=%async_computation.3 | async-start | bytes 1048576 | tf_op jit(solution)/shard_map/all_to_all | solution.py:80
  324.6 1.5 reduce.27
  326.8 5.0 %all-to-all-done.3 = bf16[1,7,64,512]{3,1,0,2:T(8,128)(2,1)S(1)} async-done(((bf16[1,7,64,512]{3,1,0,2:T(8,128)(2,1)}), bf16[1,7,64,512]{3,1,0,2:T(8,128)(2,1)S(1)}, u32[]{:S(2)}, u32[]{:S(2)}) %all-to-all-start.3) | async-done | bytes 458784 | tf_op jit(solution)/shard_map/all_to_all | solution.py:80
  331.8 5.6 %all-to-all-start.9 = ((bf16[64,2,448]{2,1,0:T(2,128)(2,1)}), bf16[64,2,448]{2,1,0:T(2,128)(2,1)S(1)}, u32[]{:S(2)}, u32[]{:S(2)}) async-start(bf16[64,2,448]{2,1,0:T(2,128)(2,1)} %reshape.403), calls=%async_computation.9 | async-start | bytes 262144 | tf_op jit(solution)/shard_map/all_to_all | solution.py:115
  338.4 14.1 %all-to-all-done.9 = bf16[64,2,448]{2,1,0:T(2,128)(2,1)S(1)} async-done(((bf16[64,2,448]{2,1,0:T(2,128)(2,1)}), bf16[64,2,448]{2,1,0:T(2,128)(2,1)S(1)}, u32[]{:S(2)}, u32[]{:S(2)}) %all-to-all-start.9) | async-done | bytes 114720 | tf_op jit(solution)/shard_map/all_to_all | solution.py:115
  354.7 16.0 %all-gather.1 = f32[8,448,7]{1,2,0:T(8,128)S(1)} all-gather(f32[1,448,7]{1,2,0:T(8,128)S(1)} %bitcast.218), channel_id=1, replica_groups=mesh['expert'=64,'context'=4,'pipe'=2] {'context','pipe'}, dimensions={0}, use_global_device_ids=true | all-gather | bytes 112896 | tf_op jit(solution)/shard_map/all_gather | solution.py:120
  (168 shorter events, 34.8 us)
Async XLA Ops:
  7.2 81.3 %copy-start = (bf16[1,128,3584]{2,1,0:T(8,128)(2,1)S(1)}, bf16[1,128,3584]{2,1,0:T(8,128)(2,1)}, u32[]{:S(2)}) copy-start(bf16[1,128,3584]{2,1,0:T(8,128)(2,1)} %param.23) | copy-start | bytes 2752516
  7.2 121.5 %reduce-scatter.7.cloned.1.call-start = ((), (), s32[]{:S(2)}) async-start(), calls=%async_computation.12 | async-start | bytes 1032192
  9.4 2.1 copy-start.19
  9.4 2.2 copy-start.6
  11.3 171.3 %copy-start.4 = (bf16[1,7,3584]{2,0,1:T(2,128)(2,1)}, bf16[1,7,3584]{2,0,1:T(2,128)(2,1)S(1)}, u32[]{:S(2)}) copy-start(bf16[1,7,3584]{2,0,1:T(2,128)(2,1)S(1)} %get-tuple-element.21) | copy-start | bytes 150532
  11.6 171.0 %copy-start.9 = (f32[3584]{0:T(1024)}, f32[3584]{0:T(1024)S(1)}, u32[]{:S(2)}) copy-start(f32[3584]{0:T(1024)S(1)} %get-tuple-element.11) | copy-start | bytes 43012
  11.6 171.0 %copy-start.11 = (f32[3584]{0:T(1024)}, f32[3584]{0:T(1024)S(1)}, u32[]{:S(2)}) copy-start(f32[3584]{0:T(1024)S(1)} %get-tuple-element.12) | copy-start | bytes 43012
  95.5 52.3 %copy-start.22 = (f32[2,7,8]{2,0,1:T(2,128)S(1)}, f32[2,7,8]{2,0,1:T(2,128)}, u32[]{:S(2)}) copy-start(f32[2,7,8]{2,0,1:T(2,128)} %param.20) | copy-start | bytes 1348
  133.2 29.4 %all-to-all-start.7 = ((bf16[64,2,448]{2,1,0:T(2,128)(2,1)}), bf16[64,2,448]{2,1,0:T(2,128)(2,1)S(1)}, u32[]{:S(2)}, u32[]{:S(2)}) async-start(bf16[64,2,448]{2,1,0:T(2,128)(2,1)} %reshape.401), calls=%async_computation.7 | async-start | bytes 262144 | tf_op jit(solution)/shard_map/all_to_all | solution.py:115
  147.7 35.0 %copy-start.23 = (f32[7]{0:T(128)}, f32[7]{0:T(128)S(1)}, u32[]{:S(2)}) copy-start(f32[7]{0:T(128)S(1)} %add_rsqrt_fusion) | copy-start | bytes 88
  182.7 16.5 %copy-start.25 = (f32[7]{0:T(128)}, f32[7]{0:T(128)S(1)}, u32[]{:S(2)}) copy-start(f32[7]{0:T(128)S(1)} %add_rsqrt_fusion.1) | copy-start | bytes 88
  199.2 4.8 %copy-start.27 = (s32[7]{0:T(128)S(1)}, s32[7]{0:T(128)}, u32[]{:S(2)}) copy-start(s32[7]{0:T(128)} %param.18) | copy-start | bytes 88
  199.2 5.5 %copy-start.1 = (bf16[7,128,576]{1,2,0:T(8,128)(2,1)S(1)}, bf16[7,128,576]{1,2,0:T(8,128)(2,1)}, u32[]{:S(2)}) copy-start(bf16[7,128,576]{1,2,0:T(8,128)(2,1)} %param.17) | copy-start | bytes 3096580
  199.2 53.0 %all-to-all-start.8 = ((bf16[64,2,3584]{2,1,0:T(2,128)(2,1)}), bf16[64,2,3584]{2,1,0:T(2,128)(2,1)S(1)}, u32[]{:S(2)}, u32[]{:S(2)}) async-start(bf16[64,2,3584]{2,1,0:T(2,128)(2,1)} %scatter_fusion.1), calls=%async_computation.8 | async-start | bytes 1835008 | tf_op jit(solution)/shard_map/all_to_all | solution.py:106
  252.2 6.2 %copy-start.3 = (bf16[64,2,3584]{2,1,0:T(2,128)(2,1)}, bf16[64,2,3584]{2,1,0:T(2,128)(2,1)S(1)}, u32[]{:S(2)}) copy-start(bf16[64,2,3584]{2,1,0:T(2,128)(2,1)S(1)} %all-to-all-done.8) | copy-start | bytes 2752516
  252.2 23.9 %all-to-all-start.1 = ((bf16[1,7,64]{1,0,2:T(2,128)(2,1)}), bf16[1,7,64]{1,0,2:T(2,128)(2,1)}, u32[]{:S(2)}, u32[]{:S(2)}) async-start(bf16[1,7,64]{1,0,2:T(2,128)(2,1)} %copy.188), calls=%async_computation.1 | async-start | bytes 65536 | tf_op jit(solution)/shard_map/all_to_all | solution.py:66
  258.4 64.4 %reduce-scatter.9.cloned.1.call-start = ((), (), s32[]{:S(2)}) async-start(), calls=%async_computation.13 | async-start | bytes 1032192
  270.9 2.6 copy-start.18
  274.9 6.5 %copy-start.20 = (s32[7,8]{1,0:T(8,128)S(1)}, s32[7,8]{1,0:T(8,128)}, u32[]{:S(2)}) copy-start(s32[7,8]{1,0:T(8,128)} %get-tuple-element.15) | copy-start | bytes 676
  276.1 9.9 %all-to-all-start.2 = ((bf16[1,7,64]{1,0,2:T(2,128)(2,1)}), bf16[1,7,64]{1,0,2:T(2,128)(2,1)S(1)}, u32[]{:S(2)}, u32[]{:S(2)}) async-start(bf16[1,7,64]{1,0,2:T(2,128)(2,1)} %copy.191), calls=%async_computation.2 | async-start | bytes 65536 | tf_op jit(solution)/shard_map/all_to_all | solution.py:73
  286.0 9.7 %all-to-all-start.5 = ((bf16[1,7,64]{1,0,2:T(2,128)(2,1)}), bf16[1,7,64]{1,0,2:T(2,128)(2,1)S(1)}, u32[]{:S(2)}, u32[]{:S(2)}) async-start(bf16[1,7,64]{1,0,2:T(2,128)(2,1)} %copy.198), calls=%async_computation.5 | async-start | bytes 65536 | tf_op jit(solution)/shard_map/all_to_all | solution.py:73
  295.6 8.7 %all-to-all-start.4 = ((bf16[1,7,64]{1,0,2:T(2,128)(2,1)}), bf16[1,7,64]{1,0,2:T(2,128)(2,1)S(1)}, u32[]{:S(2)}, u32[]{:S(2)}) async-start(bf16[1,7,64]{1,0,2:T(2,128)(2,1)} %copy.195), calls=%async_computation.4 | async-start | bytes 65536 | tf_op jit(solution)/shard_map/all_to_all | solution.py:66
  304.4 13.6 %all-to-all-start = ((bf16[1,7,64,512]{3,1,0,2:T(8,128)(2,1)}), bf16[1,7,64,512]{3,1,0,2:T(8,128)(2,1)S(1)}, u32[]{:S(2)}, u32[]{:S(2)}) async-start(bf16[1,7,64,512]{3,1,0,2:T(8,128)(2,1)} %copy.187), calls=%async_computation | async-start | bytes 1048576 | tf_op jit(solution)/shard_map/all_to_all | solution.py:80
  318.0 13.8 %all-to-all-start.3 = ((bf16[1,7,64,512]{3,1,0,2:T(8,128)(2,1)}), bf16[1,7,64,512]{3,1,0,2:T(8,128)(2,1)S(1)}, u32[]{:S(2)}, u32[]{:S(2)}) async-start(bf16[1,7,64,512]{3,1,0,2:T(8,128)(2,1)} %copy.194), calls=%async_computation.3 | async-start | bytes 1048576 | tf_op jit(solution)/shard_map/all_to_all | solution.py:80
  331.8 20.7 %all-to-all-start.9 = ((bf16[64,2,448]{2,1,0:T(2,128)(2,1)}), bf16[64,2,448]{2,1,0:T(2,128)(2,1)S(1)}, u32[]{:S(2)}, u32[]{:S(2)}) async-start(bf16[64,2,448]{2,1,0:T(2,128)(2,1)} %reshape.403), calls=%async_computation.9 | async-start | bytes 262144 | tf_op jit(solution)/shard_map/all_to_all | solution.py:115
  352.7 1.9 copy-start.21
  353.4 17.5 %copy-start.5 = (bf16[1,7,3584]{2,0,1:T(2,128)(2,1)S(1)}, bf16[1,7,3584]{2,0,1:T(2,128)(2,1)}, u32[]{:S(2)}) copy-start(bf16[1,7,3584]{2,0,1:T(2,128)(2,1)} %copy-done.4) | copy-start | bytes 150532
  353.4 17.5 %copy-start.8 = (bf16[7,3584]{1,0:T(8,128)(2,1)S(1)}, bf16[7,3584]{1,0:T(8,128)(2,1)}, u32[]{:S(2)}) copy-start(bf16[7,3584]{1,0:T(8,128)(2,1)} %copy-done.7) | copy-start | bytes 150532
  353.4 17.5 %copy-start.10 = (f32[3584]{0:T(1024)S(1)}, f32[3584]{0:T(1024)}, u32[]{:S(2)}) copy-start(f32[3584]{0:T(1024)} %copy-done.9) | copy-start | bytes 43012
  353.4 17.5 %copy-start.12 = (f32[3584]{0:T(1024)S(1)}, f32[3584]{0:T(1024)}, u32[]{:S(2)}) copy-start(f32[3584]{0:T(1024)} %copy-done.11) | copy-start | bytes 43012
  353.4 17.5 %copy-start.24 = (f32[7]{0:T(128)S(1)}, f32[7]{0:T(128)}, u32[]{:S(2)}) copy-start(f32[7]{0:T(128)} %copy-done.23) | copy-start | bytes 88
  353.5 17.5 %copy-start.26 = (f32[7]{0:T(128)S(1)}, f32[7]{0:T(128)}, u32[]{:S(2)}) copy-start(f32[7]{0:T(128)} %copy-done.25) | copy-start | bytes 88
  (7 other events, 7.7 us)
Sparse Core Ops, SparseCore 0:
  95.7 33.0 reduce-scatter.6
  273.6 29.1 reduce-scatter.8
where the time goes:
time: 380 us; the launch traced here: 379 us
  waiting for transfers between devices  128 us (34%)
  blocking collectives  98.7 us (26%)
  local copies, waits for them, and re-layouts  62.4 us (16%)
  starting transfers between devices  53 us (14%)
  between operations  14.8 us (4%)
  matrix products  12.9 us (3%)
  other arithmetic  8.22 us (2%)
    all_to_all x1, blocking collectives, body(): lax.all_to_all(buffer, 'expert', split_axis=0, concat_axis=1, tiled=True)  65.2 us
    all_to_all x1, waiting for transfers between devices, body(): lax.all_to_all(buffer, 'expert', split_axis=0, concat_axis=1, tiled=True)  43.6 us
    all_gather x2, blocking collectives, body(): lax.all_gather(routed_part, ('context', 'pipe'), axis=1, tiled=True)  33.5 us
    unnamed x4, waiting for transfers between devices  33.2 us
    all_to_all x2, waiting for transfers between devices, body(): lax.all_to_all(expert_sums.astype(jnp.bfloat16), 'expert', split_axis=1,...  28.3 us
    scatter x2, local copies, waits for them, and re-layouts, body(): buffer.at[chosen_ids, slot_index]  23.2 us
    all_to_all x2, starting transfers between devices, body(): lax.all_to_all(expert_sums.astype(jnp.bfloat16), 'expert', split_axis=1,...  20 us
    unnamed x72, local copies, waits for them, and re-layouts  19.8 us
  transfers between devices with their start and end apart: 11, of which 8 were waited for; matrix products, arithmetic and copies ran while one was open for 9% of the time, Pallas kernels for 0%

commit v1 on v0

v1 whole, which is shorter than its diff:
```python
import functools

import jax
import jax.numpy as jnp
from jax import lax
from jax.experimental import pallas as pl
from jax.experimental.pallas import tpu as pltpu
from jax.sharding import PartitionSpec as P

LATENT = 512
LOOPS = 2
LANES = 128
EPSILON = 1e-06
NEG_FILL = -1e30
F32 = jnp.float32
BF16 = jnp.bfloat16
MESH = pl.DeviceIdType.MESH


def iota(shape, axis):
    return lax.broadcasted_iota(jnp.int32, shape, axis)


def wait_bytes(ref, sem):
    pltpu.make_async_copy(ref, ref, sem).wait()


def kernel(
    sizes,
    hid_in, emb_in, gains_in, q_in, cache_in, lengths, ids, route_w, wg_in, wu_in, wd_in,
    att_out, hid_out,
    hid_raw, emb_raw, gains, queries, cache, w_gu, w_down,
    hidden, emb_norm, mixed, spread, gather_t, combine_t, order, disorder,
    tiles, disp, disp_got, rows_all,
    part, sib, red, red_got, stacked, back, back_got, comb,
    att_send, att_got, lse_send, lse_got,
    load_sem, disp_s, disp_r, ag_s, ag_r, fw_s, fw_r, sib_s, sib_r, rs_s, rs_r,
    back_s, back_r, comb_s, comb_r, att_s, att_r,
):
    ne, nx, rows, jb, topk, scale = sizes
    ni = ne // 2
    nn = ni * 16
    half = 2 * ni
    fx = jb * LANES
    group = 2 * nx
    me = lax.axis_index("expert")
    cx = lax.axis_index("context")
    cp = lax.axis_index("pipe")
    my_g = cx * 2 + cp

    def device_of(g):
        return (me, lax.div(g, 2), lax.rem(g, 2))

    def x_peer(k):
        return lax.rem(cx + k, nx)

    sibling = (me, cx, 1 - cp)

    pairs = [
        (hid_in, hid_raw),
        (emb_in, emb_raw),
        (gains_in, gains),
        (q_in, queries),
        (cache_in, cache),
        (wg_in, w_gu.at[:, 0:LANES]),
        (wu_in, w_gu.at[:, LANES : 2 * LANES]),
        (wd_in, w_down),
    ]
    loads = [pltpu.make_async_copy(a, b, load_sem.at[n]) for n, (a, b) in enumerate(pairs)]
    for copy in loads:
        copy.start()

    barrier = pltpu.get_barrier_semaphore()

    def greet(i, carry):
        d = 2 * i + cp

        @pl.when(d != 0)
        def _():
            pl.semaphore_signal(
                barrier, inc=1, device_id=(lax.rem(me + d, ne), cx, cp), device_id_type=MESH
            )

        return carry

    lax.fori_loop(0, ni, greet, 0)
    for k in range(1, group):
        pl.semaphore_signal(
            barrier, inc=1, device_id=device_of(lax.rem(my_g + k, group)), device_id_type=MESH
        )

    lane = iota((8, nn), 1)
    sub = iota((8, nn), 0)
    named = (me + 2 * lax.shift_right_logical(lane, 4) + cp) & (ne - 1)
    slot = (lax.shift_right_logical(lane, 3) & 1).astype(F32)
    block = lane & 7

    def route_tables(t):
        count = jnp.zeros((8, nn), F32)
        picked = jnp.zeros((8, nn), F32)
        weight = jnp.zeros((8, nn), F32)
        for r in range(rows):
            chosen = jnp.zeros((8, nn), F32)
            value = jnp.zeros((8, nn), F32)
            for k in range(topk):
                hit = named == ids[t, r, k]
                chosen = jnp.where(hit, 1.0, chosen)
                value = jnp.where(hit, route_w[t, r, k], value)
            here = jnp.logical_and(sub == r, count == slot)
            picked = jnp.where(here, chosen, picked)
            weight = jnp.where(here, value, weight)
            count = count + chosen
        high = weight.astype(BF16).astype(F32)
        low = weight - high
        zeros = jnp.zeros((LANES - 8 * jb, nn), F32)
        wide = jnp.concatenate(
            [jnp.where(block == j, picked, 0.0) for j in range(jb)] + [zeros], axis=0
        )
        gather_t[t] = jnp.transpose(wide).astype(BF16)
        pad = jnp.zeros((64 - 8 * jb, nn), F32)
        both = []
        for piece in (high, low):
            both += [jnp.where(block == j, piece, 0.0) for j in range(jb)] + [pad]
        combine_t[t] = jnp.concatenate(both, axis=0).astype(BF16)

    route_tables(0)

    def normed(values, gain):
        return values * lax.rsqrt(jnp.mean(values * values, axis=-1, keepdims=True) + EPSILON) * gain

    hidden[...] = jnp.zeros_like(hidden)
    emb_norm[...] = jnp.zeros_like(emb_norm)
    spread[...] = jnp.zeros_like(spread)
    for copy in loads[:3]:
        copy.wait()
    hidden[0:rows, :] = hid_raw[...].astype(F32)
    for t in range(LOOPS):
        emb_norm[t, 0:rows, :] = emb_raw[t].astype(F32)
    for t in range(LOOPS):
        emb_norm[t] = normed(emb_norm[t], gains[1:2, :])

    def dispatch_tiles(t):
        mixed[...] = normed(hidden[...], gains[0:1, :]) + emb_norm[t]
        for j in range(jb):
            at = pl.multiple_of(cx * fx + j * LANES, LANES)
            spread[8 * j : 8 * j + 8, :] = mixed[:, pl.ds(at, LANES)]
        disp[t] = jnp.dot(
            gather_t[t], spread[...].astype(BF16), preferred_element_type=F32
        ).astype(BF16)

    def exchange(t, src, dst, send_sem, recv_sem, sign):
        def send(i, carry):
            d = 2 * i + cp
            at = pl.ds(pl.multiple_of(i * 16, 16), 16)

            @pl.when(d != 0)
            def _():
                pltpu.make_async_remote_copy(
                    src_ref=src.at[t, at, :],
                    dst_ref=dst.at[t, at, :],
                    send_sem=send_sem.at[t],
                    recv_sem=recv_sem.at[t],
                    device_id=(lax.rem(me + sign * d + ne, ne), cx, cp),
                    device_id_type=MESH,
                ).start()

            @pl.when(d == 0)
            def _():
                pltpu.make_async_copy(src.at[t, at, :], dst.at[t, at, :], recv_sem.at[t]).start()

            return carry

        lax.fori_loop(0, ni, send, 0)

    def exchange_sent(t, src, send_sem):
        wait_bytes(src.at[t, 16:nn, :], send_sem.at[t])

        @pl.when(cp == 1)
        def _():
            wait_bytes(src.at[t, 0:16, :], send_sem.at[t])

    def reorder_tables():
        m = iota((jb * half, nn), 0)
        n = iota((jb * half, nn), 1)
        s_i = lax.rem(m, half)
        want = lax.rem(s_i, ni) * 16 + lax.div(s_i, ni) * 8 + lax.div(m, half)
        order[...] = jnp.where(n == want, 1.0, 0.0).astype(BF16)
        n = iota((nn, jb * half), 0)
        m = iota((nn, jb * half), 1)
        s_i = lax.rem(m, half)
        want = lax.rem(s_i, ni) * 16 + lax.div(s_i, ni) * 8 + lax.div(m, half)
        disorder[...] = jnp.where(n == want, 1.0, 0.0).astype(BF16)

    def attention_partials():
        heads = queries.shape[2]
        position = my_g * LANES + iota((2 * heads, LANES), 1)
        column = iota((2 * heads, LANES), 1)
        lse_all = jnp.zeros((2 * heads, LANES), F32)
        for r in range(rows):
            q = jnp.concatenate([queries[0, r], queries[1, r]], axis=0)
            keys = cache[r]
            scores = lax.dot_general(
                q, keys, (((1,), (1,)), ((), ())), preferred_element_type=F32
            ) * scale
            live = position < lengths[r]
            scores = jnp.where(live, scores, NEG_FILL)
            top = jnp.max(scores, axis=-1, keepdims=True)
            weights = jnp.where(live, jnp.exp(scores - top), 0.0).astype(BF16)
            total = jnp.sum(weights.astype(F32), axis=-1, keepdims=True)
            summed = jnp.dot(weights, keys[:, :LATENT], preferred_element_type=F32)
            some = total > 0.0
            safe = jnp.where(some, total, 1.0)
            mean = summed / safe
            lse = jnp.where(some, top + jnp.log(safe), NEG_FILL)
            lse_all = jnp.where(column == r, lse, lse_all)
            for g in range(group):
                att_send[g, 16 * r : 16 * r + 16, :] = jnp.concatenate(
                    [mean[8 * g : 8 * g + 8], mean[heads + 8 * g : heads + 8 * g + 8]], axis=0
                ).astype(BF16)
        for g in range(group):
            lse_send[g] = jnp.concatenate(
                [lse_all[8 * g : 8 * g + 8], lse_all[heads + 8 * g : heads + 8 * g + 8]], axis=0
            )

    def attention_copies(k):
        to = lax.rem(my_g + k, group)
        return [
            pltpu.make_async_remote_copy(
                src_ref=a.at[to],
                dst_ref=b.at[k - 1],
                send_sem=att_s.at[n, k - 1],
                recv_sem=att_r.at[n, k - 1],
                device_id=device_of(to),
                device_id_type=MESH,
            )
            for n, (a, b) in enumerate(((att_send, att_got), (lse_send, lse_got)))
        ]

    def attention_send(ks):
        for k in ks:
            for copy in attention_copies(k):
                copy.start()

    def attention_finish():
        for k in range(1, group):
            for copy in attention_copies(k):
                copy.wait()
        for r in range(rows):
            tops = [lse_send[my_g][:, r : r + 1]]
            tops += [lse_got[k][:, r : r + 1] for k in range(group - 1)]
            best = functools.reduce(jnp.maximum, tops)
            factors = [jnp.exp(top - best) for top in tops]
            share = 1.0 / functools.reduce(jnp.add, factors)
            at = slice(16 * r, 16 * r + 16)
            total = att_send[my_g, at, :].astype(F32) * (factors[0] * share)
            for k in range(group - 1):
                total += att_got[k, at, :].astype(F32) * (factors[k + 1] * share)
            for t in range(LOOPS):
                att_out[t, r] = total[8 * t : 8 * t + 8].astype(BF16)

    own_rows = pl.ds(pl.multiple_of(cp * half, half), half)
    other_rows = pl.ds(pl.multiple_of((1 - cp) * half, half), half)

    def gather_copy(t, k):
        at = rows_all.at[t, cx, own_rows, :]
        if k == 0:
            return pltpu.make_async_remote_copy(
                src_ref=at, dst_ref=at, send_sem=fw_s.at[t, 0], recv_sem=fw_r.at[t, 0],
                device_id=sibling, device_id_type=MESH,
            )
        return pltpu.make_async_remote_copy(
            src_ref=at, dst_ref=at, send_sem=ag_s.at[t, k - 1], recv_sem=ag_r.at[t, k - 1],
            device_id=(me, x_peer(k), cp), device_id_type=MESH,
        )

    def forward_copy(t, k):
        at = rows_all.at[t, x_peer(nx - k), own_rows, :]
        return pltpu.make_async_remote_copy(
            src_ref=at, dst_ref=at, send_sem=fw_s.at[t, k], recv_sem=fw_r.at[t, k],
            device_id=sibling, device_id_type=MESH,
        )

    def sibling_copy(t, k):
        return pltpu.make_async_remote_copy(
            src_ref=part.at[t, k, other_rows, :], dst_ref=sib.at[t, k],
            send_sem=sib_s.at[t, k], recv_sem=sib_r.at[t, k],
            device_id=sibling, device_id_type=MESH,
        )

    def reduce_copy(t, k):
        return pltpu.make_async_remote_copy(
            src_ref=red.at[t, k - 1], dst_ref=red_got.at[t, k - 1],
            send_sem=rs_s.at[t, k - 1], recv_sem=rs_r.at[t, k - 1],
            device_id=(me, x_peer(k), cp), device_id_type=MESH,
        )

    def combine_copy(t, k):
        at = comb.at[t, my_g]
        return pltpu.make_async_remote_copy(
            src_ref=at, dst_ref=at,
            send_sem=comb_s.at[t, k - 1], recv_sem=comb_r.at[t, k - 1],
            device_id=device_of(lax.rem(my_g + k, group)), device_id_type=MESH,
        )

    near_first = [k for k in range(1, nx) if k in (1, nx - 1)]
    near_first += [k for k in range(1, nx) if k not in (1, nx - 1)]
    far_first = near_first[::-1]

    dispatch_tiles(0)
    pl.semaphore_wait(barrier, ni - 1 + cp + group - 1)

    for t in range(LOOPS):
        exchange(t, disp, disp_got, disp_s, disp_r, 1)
        if t == 0:
            reorder_tables()
            for copy in loads[3:5]:
                copy.wait()
            attention_partials()
            for copy in loads[5:]:
                copy.wait()
        else:
            attention_send([k for k in range(1, group) if k % 2 == 0])
        wait_bytes(disp_got.at[t], disp_r.at[t])
        got = jnp.dot(order[...], disp_got[t], preferred_element_type=F32).astype(BF16)
        for j in range(jb):
            rows_all[t, cx, own_rows, j * LANES : (j + 1) * LANES] = got[half * j : half * j + half]
        for k in [0] + near_first:
            gather_copy(t, k).start()
        total = jnp.zeros((2 * half, 2 * LANES), F32)
        for k in [0] + near_first:
            if k:
                gather_copy(t, k).wait_recv()
                forward_copy(t, k).start()
        for k in [0] + near_first:
            forward_copy(t, k).wait_recv()
            at = x_peer(nx - k) if k else cx
            total += jnp.dot(
                rows_all[t, at],
                w_gu[pl.ds(pl.multiple_of(at * fx, LANES), fx), :],
                preferred_element_type=F32,
            )
        gate, up = total[:, :LANES], total[:, LANES:]
        active = (gate * (1.0 / (1.0 + jnp.exp(-gate))) * up).astype(BF16)
        for k in far_first + [0]:
            at = pl.multiple_of(x_peer(k) * fx, LANES)
            part[t, k] = jnp.dot(
                active, w_down[:, pl.ds(at, fx)], preferred_element_type=F32
            ).astype(BF16)
            sibling_copy(t, k).start()
        for k in far_first:
            sibling_copy(t, k).wait_recv()
            red[t, k - 1] = (
                part[t, k, own_rows, :].astype(F32) + sib[t, k].astype(F32)
            ).astype(BF16)
            reduce_copy(t, k).start()
        sibling_copy(t, 0).wait_recv()
        summed = part[t, 0, own_rows, :].astype(F32) + sib[t, 0].astype(F32)
        for k in near_first:
            reduce_copy(t, k).wait_recv()
            summed += red_got[t, k - 1].astype(F32)
        for j in range(jb):
            stacked[half * j : half * j + half, :] = summed[:, j * LANES : (j + 1) * LANES].astype(BF16)
        back[t] = jnp.dot(disorder[...], stacked[...], preferred_element_type=F32).astype(BF16)
        exchange(t, back, back_got, back_s, back_r, -1)
        if t == 0:
            attention_send([k for k in range(1, group) if k % 2 == 1])
            route_tables(1)
        else:
            attention_finish()
        wait_bytes(back_got.at[t], back_r.at[t])
        routed = jnp.dot(combine_t[t], back_got[t], preferred_element_type=F32)
        comb[t, my_g] = (routed[0:64] + routed[64:128]).astype(BF16)
        for k in range(1, group):
            combine_copy(t, k).start()
        for k in range(1, group):
            combine_copy(t, k).wait_recv()
        for x in range(nx):
            pair = comb[t, 2 * x].astype(F32) + comb[t, 2 * x + 1].astype(F32)
            for j in range(jb):
                at = slice(x * fx + j * LANES, x * fx + (j + 1) * LANES)
                hidden[:, at] = (mixed[:, at] + pair[8 * j : 8 * j + 8]).astype(BF16).astype(F32)
        if t + 1 < LOOPS:
            dispatch_tiles(t + 1)
    hid_out[...] = hidden[0:rows, :].astype(BF16)

    for t in range(LOOPS):
        exchange_sent(t, disp, disp_s)
        exchange_sent(t, back, back_s)
        for k in range(nx):
            forward_copy(t, k).wait_send()
            sibling_copy(t, k).wait_send()
            if k:
                gather_copy(t, k).wait_send()
                reduce_copy(t, k).wait_send()
        for k in range(1, group):
            combine_copy(t, k).wait_send()


def body(
    ne, nx,
    hidden_in, draft_embeds, norm_gains, queries, latent_cache, lengths, route_ids, route_weights,
    w_gate, w_up, w_down,
):
    rows, width = hidden_in.shape
    topk = route_ids.shape[2]
    fx = width // nx
    jb = fx // LANES
    ni = ne // 2
    nn = 16 * ni
    half = 2 * ni
    group = 2 * nx
    sizes = (ne, nx, rows, jb, topk, float(queries.shape[3]) ** (-0.5))
    any_spec = pl.BlockSpec(memory_space=pl.ANY)
    smem = pl.BlockSpec(memory_space=pltpu.SMEM)
    vmem = pl.BlockSpec(memory_space=pltpu.VMEM)
    dma = pltpu.SemaphoreType.DMA
    scratch = [
        pltpu.VMEM(hidden_in.shape, BF16),
        pltpu.VMEM(draft_embeds.shape, BF16),
        pltpu.VMEM(norm_gains.shape, F32),
        pltpu.VMEM(queries.shape, BF16),
        pltpu.VMEM(latent_cache.shape, BF16),
        pltpu.VMEM((width, 2 * LANES), BF16),
        pltpu.VMEM(w_down.shape[1:], BF16),
        pltpu.VMEM((8, width), F32),
        pltpu.VMEM((LOOPS, 8, width), F32),
        pltpu.VMEM((8, width), F32),
        pltpu.VMEM((LANES, LANES), F32),
        pltpu.VMEM((LOOPS, nn, LANES), BF16),
        pltpu.VMEM((LOOPS, LANES, nn), BF16),
        pltpu.VMEM((jb * half, nn), BF16),
        pltpu.VMEM((nn, jb * half), BF16),
        pltpu.VMEM((8, LANES), F32),
        pltpu.VMEM((LOOPS, nn, LANES), BF16),
        pltpu.VMEM((LOOPS, nn, LANES), BF16),
        pltpu.VMEM((LOOPS, nx, 2 * half, fx), BF16),
        pltpu.VMEM((LOOPS, nx, 2 * half, fx), BF16),
        pltpu.VMEM((LOOPS, nx, half, fx), BF16),
        pltpu.VMEM((LOOPS, nx - 1, half, fx), BF16),
        pltpu.VMEM((LOOPS, nx - 1, half, fx), BF16),
        pltpu.VMEM((jb * half, LANES), BF16),
        pltpu.VMEM((LOOPS, nn, LANES), BF16),
        pltpu.VMEM((LOOPS, nn, LANES), BF16),
        pltpu.VMEM((LOOPS, group, 64, LANES), BF16),
        pltpu.VMEM((group, 16 * rows, LATENT), BF16),
        pltpu.VMEM((group - 1, 16 * rows, LATENT), BF16),
        pltpu.VMEM((group, 16, LANES), F32),
        pltpu.VMEM((group - 1, 16, LANES), F32),
        dma((8,)),
        dma((LOOPS,)), dma((LOOPS,)),
        dma((LOOPS, nx - 1)), dma((LOOPS, nx - 1)),
        dma((LOOPS, nx)), dma((LOOPS, nx)),
        dma((LOOPS, nx)), dma((LOOPS, nx)),
        dma((LOOPS, nx - 1)), dma((LOOPS, nx - 1)),
        dma((LOOPS,)), dma((LOOPS,)),
        dma((LOOPS, group - 1)), dma((LOOPS, group - 1)),
        dma((2, group - 1)), dma((2, group - 1)),
    ]
    heads_here = queries.shape[2] // group
    return tuple(
        pl.pallas_call(
            functools.partial(kernel, sizes),
            out_shape=(
                jax.ShapeDtypeStruct((LOOPS, rows, heads_here, LATENT), BF16),
                jax.ShapeDtypeStruct((rows, width), BF16),
            ),
            in_specs=[any_spec] * 5 + [smem] * 3 + [any_spec] * 3,
            out_specs=(vmem, vmem),
            scratch_shapes=scratch,
            compiler_params=pltpu.CompilerParams(
                collective_id=0, has_side_effects=True, vmem_limit_bytes=40 * 1024 * 1024
            ),
            name="draft_steps",
        )(
            hidden_in, draft_embeds, norm_gains, queries, latent_cache, lengths, route_ids,
            route_weights, w_gate[0], w_up[0], w_down[0],
        )
    )


def solution(mesh):
    in_specs = (
        P("expert", None),
        P(None, "expert", None),
        P(),
        P(None, "expert", None, None),
        P("expert", ("context", "pipe"), None),
        P("expert"),
        P(None, "expert", None),
        P(None, "expert", None),
        P("expert", None, ("context", "pipe")),
        P("expert", None, ("context", "pipe")),
        P("expert", ("context", "pipe"), None),
    )
    out_specs = (P(None, "expert", ("context", "pipe"), None), P("expert", None))
    run = functools.partial(body, mesh.shape["expert"], mesh.shape["context"])
    return jax.shard_map(run, mesh=mesh, in_specs=in_specs, out_specs=out_specs, check_vma=False)
```

time: 380 us -> 119 us (0.31)
  waiting for transfers between devices: 128 us -> 0 us
  Pallas kernels: 0 us -> 110 us
  blocking collectives: 98.7 us -> 0 us
  local copies, waits for them, and re-layouts: 62.4 us -> 8.12 us
  starting transfers between devices: 53 us -> 0 us
  between operations: 14.8 us -> 0.71 us
  matrix products: 12.9 us -> 0 us
  other arithmetic: 8.22 us -> 0 us
    pallas_call x0 -> x1, Pallas kernels: none -> 110 us  [body(): pl.pallas_call(functools.partial(kernel, sizes), out_shape=(jax.ShapeDtyp...]
    all_to_all x9 -> x0, waiting for transfers between devices: 95.3 us -> none  [the longest x1 43.6 us: body(): lax.all_to_all(buffer, 'expert', split_axis=0, concat_axis=1, tiled=True)]
    all_to_all x1 -> x0, blocking collectives: 65.2 us -> none  [body(): lax.all_to_all(buffer, 'expert', split_axis=0, concat_axis=1, tiled=True)]
    all_to_all x9 -> x0, starting transfers between devices: 53 us -> none  [the longest x2 20 us: body(): lax.all_to_all(expert_sums.astype(jnp.bfloat16), 'expert', split_axis=1,...]
    all_gather x2 -> x0, blocking collectives: 33.5 us -> none  [body(): lax.all_gather(routed_part, ('context', 'pipe'), axis=1, tiled=True)]
    unnamed x4 -> x0, waiting for transfers between devices: 33.2 us -> none
    scatter x2 -> x0, local copies, waits for them, and re-layouts: 23.2 us -> none  [body(): buffer.at[chosen_ids, slot_index]]
    dot_general x8 -> x0, matrix products: 12.9 us -> none  [the longest x2 4.51 us: body(): jnp.einsum('emf,efd->emd', active, w_down, preferred_element_type=jnp.flo...]
  transfers between devices with their start and end apart: 11 -> 0, of which waited for: 8 -> 0; matrix products, arithmetic and copies ran while one was open for 9% -> 0% of each run, Pallas kernels for 0% -> 0%
where the time goes in v1:
time: 119 us
  Pallas kernels  110 us (92%)
  local copies, waits for them, and re-layouts  8.12 us (7%)
    pallas_call x1, Pallas kernels, body(): pl.pallas_call(functools.partial(kernel, sizes), out_shape=(jax.ShapeDtyp...  110 us
    unnamed x20, local copies, waits for them, and re-layouts  8.12 us

profile of v1, /device:TPU:1, one launch (start us, length us, event | category | flops | bytes accessed | tf_op | source)
XLA Modules:
  0.0 118.8 jit_solution(4052557050589888857)
XLA Ops:
  0.6 0.7 copy.15.ids
  1.3 0.7 copy.16.route_w
  2.0 0.0 copy-start
  2.0 0.0 copy-start.1
  2.0 0.0 copy-start.4
  2.0 0.0 copy-start.5
  2.0 0.0 copy-start.6
  2.0 1.1 copy.13.emb_in
  3.1 2.0 %copy.14.cache_in = bf16[7,128,576]{2,1,0:T(8,128)(2,1)S(1)} copy(bf16[7,128,576]{1,2,0:T(8,128)(2,1)} %param.15) | data formatting | bytes 2064384 | tf_op args[4]
  5.1 0.0 copy-done
  5.2 0.0 copy-done.1
  5.2 0.0 copy-done.4
  5.2 0.0 copy-done.5
  5.2 0.0 copy-done.6
  5.2 0.0 copy-start.2
  5.2 1.2 copy-done.2
  6.4 0.0 copy-start.3
  6.4 1.2 copy-done.3
  7.6 110.0 %draft_steps.1 = (bf16[2,7,8,512]{3,2,1,0:T(8,128)(2,1)S(1)}, bf16[7,3584]{1,0:T(8,128)(2,1)S(1)}) custom-call(bf16[7,3584]{1,0:T(8,128)(2,1)S(1)} %copy-done.4, bf16[2,7,3584]{2,1,0:T(8,128)(2,1)S(1)} %copy.13.emb_in, f32[2,3584]{1,0:T(2,128)S(1)} %copy-done.5, bf16[2,7,64,576]{3,2,1,0:T(8,128)(2,1)S(1)} %copy-done, ...), custom_call_target="tpu_custom_call" | custom-call | tf_op jit(solution)/shard_map/draft_steps/pallas_call | solution.py:461
  117.5 0.6 copy.19
  118.2 0.6 copy.20
Async XLA Ops:
  2.0 3.1 %copy-start = (bf16[2,7,64,576]{3,2,1,0:T(8,128)(2,1)S(1)}, bf16[2,7,64,576]{3,2,1,0:T(8,128)(2,1)}, u32[]{:S(2)}) copy-start(bf16[2,7,64,576]{3,2,1,0:T(8,128)(2,1)} %q_in.1) | copy-start | bytes 3096580
  2.0 3.1 %copy-start.1 = (bf16[1,3584,128]{2,1,0:T(8,128)(2,1)S(1)}, bf16[1,3584,128]{2,1,0:T(8,128)(2,1)}, u32[]{:S(2)}) copy-start(bf16[1,3584,128]{2,1,0:T(8,128)(2,1)} %param.19) | copy-start | bytes 2752516
  2.0 3.1 %copy-start.4 = (bf16[7,3584]{1,0:T(8,128)(2,1)S(1)}, bf16[7,3584]{1,0:T(8,128)(2,1)}, u32[]{:S(2)}) copy-start(bf16[7,3584]{1,0:T(8,128)(2,1)} %hid_in.1) | copy-start | bytes 150532
  2.0 3.1 %copy-start.5 = (f32[2,3584]{1,0:T(2,128)S(1)}, f32[2,3584]{1,0:T(2,128)}, u32[]{:S(2)}) copy-start(f32[2,3584]{1,0:T(2,128)} %gains_in.1) | copy-start | bytes 86020
  2.0 3.2 %copy-start.6 = (s32[7]{0:T(128)S(1)}, s32[7]{0:T(128)}, u32[]{:S(2)}) copy-start(s32[7]{0:T(128)} %lengths.1) | copy-start | bytes 88
  5.2 1.2 copy-start.2
  6.4 1.2 copy-start.3

commit v2 on v1

v2 whole, which is shorter than its diff:
```python
import functools

import jax
import jax.numpy as jnp
from jax import lax
from jax.experimental import pallas as pl
from jax.experimental.pallas import tpu as pltpu
from jax.sharding import PartitionSpec as P

LATENT = 512
LOOPS = 2
LANES = 128
EPSILON = 1e-06
NEG_FILL = -1e30
CHUNKS = (16, 16)
PLAN = ("A0", "A1", "C0", "C1", "E0", "E1")
F32 = jnp.float32
BF16 = jnp.bfloat16
MESH = pl.DeviceIdType.MESH


def iota(shape, axis):
    return lax.broadcasted_iota(jnp.int32, shape, axis)


def tile_offset(n, ni):
    step = lax.shift_right_logical(n + 1, 1)
    return jnp.where((n & 1) == 0, step, ni - step)


def wait_bytes(ref, sem):
    pltpu.make_async_copy(ref, ref, sem).wait()


def kernel(
    sizes,
    hid_in, emb_in, gains_in, q_in, cache_in, lengths_in, ids_in, route_w_in, wg_in, wu_in, wd_in,
    att_out, hid_out,
    lengths, ids, route_w, hid_raw, emb_raw, gains, queries, cache, w_gu, w_down,
    hidden, emb_norm, mixed, spread, gather_t, combine_t, order, disorder,
    disp, disp_got, rows_all,
    part, red_got, stacked, back, back_got, comb,
    att_send, att_got, lse_send, lse_got,
    scalar_sem, load_sem, w_s, w_r, disp_s, disp_r, ag_s, ag_r, rs_s, rs_r,
    back_s, back_r, comb_s, comb_r, att_s, att_r,
):
    ne, nx, rows, jb, topk, scale = sizes
    ni = ne // 2
    nn = ni * 16
    first = [sum(CHUNKS[:c]) for c in range(len(CHUNKS) + 1)]
    spans = [slice(16 * a, 16 * b) for a, b in zip(first, first[1:])]
    halves = [2 * n for n in CHUNKS]
    fx = jb * LANES
    group = 2 * nx
    me = lax.axis_index("expert")
    cx = lax.axis_index("context")
    cp = lax.axis_index("pipe")
    my_g = cx * 2 + cp

    def device_of(g):
        return (me, lax.div(g, 2), lax.rem(g, 2))

    def x_peer(k):
        return lax.rem(cx + k, nx)

    sibling = (me, cx, 1 - cp)

    barrier = pltpu.get_barrier_semaphore()

    def greet(n, carry):
        d = 2 * tile_offset(ni - 1 - n, ni) + cp

        @pl.when(d != 0)
        def _():
            pl.semaphore_signal(
                barrier, inc=1, device_id=(lax.rem(me + d, ne), cx, cp), device_id_type=MESH
            )

        return carry

    lax.fori_loop(0, ni, greet, 0)
    for k in range(1, group):
        pl.semaphore_signal(
            barrier, inc=1, device_id=device_of(lax.rem(my_g + k, group)), device_id_type=MESH
        )

    scalars = [
        pltpu.make_async_copy(a, b, scalar_sem.at[n])
        for n, (a, b) in enumerate(((ids_in, ids), (route_w_in, route_w), (lengths_in, lengths)))
    ]
    for copy in scalars:
        copy.start()
    pairs = [
        (hid_in, hid_raw),
        (emb_in, emb_raw),
        (gains_in, gains),
        (q_in, queries),
        (cache_in, cache),
        (wg_in, w_gu.at[:, 0:LANES]),
        (wu_in, w_gu.at[:, LANES : 2 * LANES]),
        (wd_in, w_down.at[0:LANES, :]),
    ]
    loads = [pltpu.make_async_copy(a, b, load_sem.at[n]) for n, (a, b) in enumerate(pairs)]
    for copy in loads:
        copy.start()

    lane = iota((8, nn), 1)
    sub = iota((8, nn), 0)
    named = (me + 2 * tile_offset(lax.shift_right_logical(lane, 4), ni) + cp) & (ne - 1)
    slot = (lax.shift_right_logical(lane, 3) & 1).astype(F32)
    block = lane & 7

    def route_tables(t):
        count = jnp.zeros((8, nn), F32)
        picked = jnp.zeros((8, nn), F32)
        weight = jnp.zeros((8, nn), F32)
        for r in range(rows):
            chosen = jnp.zeros((8, nn), F32)
            value = jnp.zeros((8, nn), F32)
            for k in range(topk):
                hit = named == ids[r, t, k]
                chosen = jnp.where(hit, 1.0, chosen)
                value = jnp.where(hit, route_w[r, t, k], value)
            here = jnp.logical_and(sub == r, count == slot)
            picked = jnp.where(here, chosen, picked)
            weight = jnp.where(here, value, weight)
            count = count + chosen
        high = weight.astype(BF16).astype(F32)
        low = weight - high
        zeros = jnp.zeros((LANES - 8 * jb, nn), F32)
        wide = jnp.concatenate(
            [jnp.where(block == j, picked, 0.0) for j in range(jb)] + [zeros], axis=0
        )
        gather_t[t] = jnp.transpose(wide).astype(BF16)
        pad = jnp.zeros((64 - 8 * jb, nn), F32)
        both = []
        for piece in (high, low):
            both += [jnp.where(block == j, piece, 0.0) for j in range(jb)] + [pad]
        combine_t[t] = jnp.concatenate(both, axis=0).astype(BF16)

    for copy in scalars:
        copy.wait()
    route_tables(0)

    def normed(values, gain):
        return values * lax.rsqrt(jnp.mean(values * values, axis=-1, keepdims=True) + EPSILON) * gain

    hidden[...] = jnp.zeros_like(hidden)
    emb_norm[...] = jnp.zeros_like(emb_norm)
    spread[...] = jnp.zeros_like(spread)
    for copy in loads[:3]:
        copy.wait()
    hidden[0:rows, :] = hid_raw[...].astype(F32)
    for t in range(LOOPS):
        emb_norm[t, 0:rows, :] = emb_raw[:, t, :].astype(F32)
    for t in range(LOOPS):
        emb_norm[t] = normed(emb_norm[t], gains[1:2, :])

    def dispatch_tiles(t):
        mixed[...] = normed(hidden[...], gains[0:1, :]) + emb_norm[t]
        for j in range(jb):
            at = pl.multiple_of(cx * fx + j * LANES, LANES)
            spread[8 * j : 8 * j + 8, :] = mixed[:, pl.ds(at, LANES)]
        disp[t] = jnp.dot(
            gather_t[t], spread[...].astype(BF16), preferred_element_type=F32
        ).astype(BF16)

    def chunk_of(n):
        return sum(jnp.where(n >= at, 1, 0) for at in first[1:-1])

    def exchange(t, last, count, src, dst, send_sem, recv_sem, sign):
        def send(m, carry):
            n = last - m
            d = 2 * tile_offset(n, ni) + cp
            at = pl.ds(pl.multiple_of(n * 16, 16), 16)
            done = recv_sem.at[t, chunk_of(n)]

            @pl.when(d != 0)
            def _():
                pltpu.make_async_remote_copy(
                    src_ref=src.at[t, at, :],
                    dst_ref=dst.at[t, at, :],
                    send_sem=send_sem.at[t],
                    recv_sem=done,
                    device_id=(lax.rem(me + sign * d + ne, ne), cx, cp),
                    device_id_type=MESH,
                ).start()

            @pl.when(d == 0)
            def _():
                pltpu.make_async_copy(src.at[t, at, :], dst.at[t, at, :], done).start()

            return carry

        lax.fori_loop(0, count, send, 0)

    def exchange_sent(t, src, send_sem):
        wait_bytes(src.at[t, 16:nn, :], send_sem.at[t])

        @pl.when(cp == 1)
        def _():
            wait_bytes(src.at[t, 0:16, :], send_sem.at[t])

    def reorder_tables():
        for c, (count, half) in enumerate(zip(CHUNKS, halves)):

            def place(m):
                s_i = lax.rem(m, half)
                return lax.rem(s_i, count) * 16 + lax.div(s_i, count) * 8 + lax.div(m, half)

            shape = (jb * half, 16 * count)
            order[c, : shape[0], : shape[1]] = jnp.where(
                iota(shape, 1) == place(iota(shape, 0)), 1.0, 0.0
            ).astype(BF16)
            shape = (16 * count, jb * half)
            disorder[c, : shape[0], : shape[1]] = jnp.where(
                iota(shape, 0) == place(iota(shape, 1)), 1.0, 0.0
            ).astype(BF16)

    def attention_partials():
        heads = queries.shape[2]
        position = my_g * LANES + iota((2 * heads, LANES), 1)
        column = iota((2 * heads, LANES), 1)
        lse_all = jnp.zeros((2 * heads, LANES), F32)
        for r in range(rows):
            q = jnp.concatenate([queries[0, r], queries[1, r]], axis=0)
            keys = cache[r]
            scores = lax.dot_general(
                q, keys, (((1,), (0,)), ((), ())), preferred_element_type=F32
            ) * scale
            live = position < lengths[r]
            scores = jnp.where(live, scores, NEG_FILL)
            top = jnp.max(scores, axis=-1, keepdims=True)
            weights = jnp.where(live, jnp.exp(scores - top), 0.0).astype(BF16)
            total = jnp.sum(weights.astype(F32), axis=-1, keepdims=True)
            summed = lax.dot_general(
                weights, keys[:LATENT], (((1,), (1,)), ((), ())), preferred_element_type=F32
            )
            some = total > 0.0
            safe = jnp.where(some, total, 1.0)
            mean = summed / safe
            lse = jnp.where(some, top + jnp.log(safe), NEG_FILL)
            lse_all = jnp.where(column == r, lse, lse_all)
            for g in range(group):
                att_send[g, 16 * r : 16 * r + 16, :] = jnp.concatenate(
                    [mean[8 * g : 8 * g + 8], mean[heads + 8 * g : heads + 8 * g + 8]], axis=0
                ).astype(BF16)
        for g in range(group):
            lse_send[g] = jnp.concatenate(
                [lse_all[8 * g : 8 * g + 8], lse_all[heads + 8 * g : heads + 8 * g + 8]], axis=0
            )

    def attention_copies(k):
        to = lax.rem(my_g + k, group)
        return [
            pltpu.make_async_remote_copy(
                src_ref=a.at[to],
                dst_ref=b.at[k - 1],
                send_sem=att_s.at[n, k - 1],
                recv_sem=att_r.at[n, k - 1],
                device_id=device_of(to),
                device_id_type=MESH,
            )
            for n, (a, b) in enumerate(((att_send, att_got), (lse_send, lse_got)))
        ]

    def attention_send(ks):
        for k in ks:
            for copy in attention_copies(k):
                copy.start()

    def attention_finish():
        for k in range(1, group):
            for copy in attention_copies(k):
                copy.wait()
        for r in range(rows):
            tops = [lse_send[my_g][:, r : r + 1]]
            tops += [lse_got[k][:, r : r + 1] for k in range(group - 1)]
            best = functools.reduce(jnp.maximum, tops)
            factors = [jnp.exp(top - best) for top in tops]
            share = 1.0 / functools.reduce(jnp.add, factors)
            at = slice(16 * r, 16 * r + 16)
            total = att_send[my_g, at, :].astype(F32) * (factors[0] * share)
            for k in range(group - 1):
                total += att_got[k, at, :].astype(F32) * (factors[k + 1] * share)
            for t in range(LOOPS):
                att_out[t, r] = total[8 * t : 8 * t + 8].astype(BF16)


    def gather_copy(t, c, k):
        at = rows_all.at[t, c, cx, 0 : halves[c], :]
        return pltpu.make_async_remote_copy(
            src_ref=at, dst_ref=at, send_sem=ag_s.at[t, c, k - 1], recv_sem=ag_r.at[t, c, k - 1],
            device_id=(me, x_peer(k), cp), device_id_type=MESH,
        )

    def reduce_copy(t, c, k):
        return pltpu.make_async_remote_copy(
            src_ref=part.at[t, c, k, 0 : halves[c], :],
            dst_ref=red_got.at[t, c, k - 1, 0 : halves[c], :],
            send_sem=rs_s.at[t, c, k - 1], recv_sem=rs_r.at[t, c, k - 1],
            device_id=(me, x_peer(k), cp), device_id_type=MESH,
        )

    def weight_copies():
        places = (
            (w_gu.at[:, 0 : 2 * LANES], w_gu.at[:, 2 * LANES : 4 * LANES]),
            (w_down.at[0:LANES, :], w_down.at[LANES : 2 * LANES, :]),
        )
        return [
            pltpu.make_async_remote_copy(
                src_ref=a, dst_ref=b, send_sem=w_s.at[n], recv_sem=w_r.at[n],
                device_id=sibling, device_id_type=MESH,
            )
            for n, (a, b) in enumerate(places)
        ]

    def combine_copy(t, k):
        at = comb.at[t, my_g]
        return pltpu.make_async_remote_copy(
            src_ref=at, dst_ref=at,
            send_sem=comb_s.at[t, k - 1], recv_sem=comb_r.at[t, k - 1],
            device_id=(me, x_peer(k // 2), 1 - cp if k % 2 else cp), device_id_type=MESH,
        )

    near_first = [k for k in range(1, nx) if k in (1, nx - 1)]
    near_first += [k for k in range(1, nx) if k not in (1, nx - 1)]
    far_first = near_first[::-1]
    others = [n for k in far_first for n in (2 * k, 2 * k + 1)] + [1]

    def stage_a(t, c):
        at, half = spans[c], halves[c]
        wait_bytes(disp_got.at[t, at, :], disp_r.at[t, c])
        got = jnp.dot(
            order[c, : jb * half, : 8 * half], disp_got[t, at, :], preferred_element_type=F32
        ).astype(BF16)
        for j in range(jb):
            rows_all[t, c, cx, 0:half, j * LANES : (j + 1) * LANES] = got[half * j : half * j + half]
        for k in far_first:
            gather_copy(t, c, k).start()

    def stage_c(t, c):
        half = halves[c]
        total = jnp.zeros((half, 4 * LANES), F32)
        for k in [0] + near_first:
            if k:
                gather_copy(t, c, k).wait_recv()
            at = x_peer(nx - k) if k else cx
            total += jnp.dot(
                rows_all[t, c, at, :half, :],
                w_gu[pl.ds(pl.multiple_of(at * fx, LANES), fx), :],
                preferred_element_type=F32,
            )
        gate = jnp.concatenate([total[:, :LANES], total[:, 2 * LANES : 3 * LANES]], axis=1)
        up = jnp.concatenate([total[:, LANES : 2 * LANES], total[:, 3 * LANES :]], axis=1)
        active = (gate * (1.0 / (1.0 + jnp.exp(-gate))) * up).astype(BF16)
        for k in far_first + [0]:
            at = pl.multiple_of(x_peer(k) * fx, LANES)
            part[t, c, k, :half, :] = jnp.dot(
                active, w_down[:, pl.ds(at, fx)], preferred_element_type=F32
            ).astype(BF16)
            if k:
                reduce_copy(t, c, k).start()

    def stage_e(t, c):
        half = halves[c]
        summed = part[t, c, 0, :half, :].astype(F32)
        for k in near_first:
            reduce_copy(t, c, k).wait_recv()
            summed += red_got[t, c, k - 1, :half, :].astype(F32)
        for j in range(jb):
            stacked[half * j : half * j + half, :] = summed[:, j * LANES : (j + 1) * LANES].astype(BF16)
        back[t, spans[c], :] = jnp.dot(
            disorder[c, : 8 * half, : jb * half], stacked[: jb * half, :], preferred_element_type=F32
        ).astype(BF16)
        exchange(t, first[c + 1] - 1, CHUNKS[c], back, back_got, back_s, back_r, -1)

    stages = {"A": stage_a, "C": stage_c, "E": stage_e}

    dispatch_tiles(0)
    reorder_tables()
    for copy in loads[3:5]:
        copy.wait()
    attention_partials()
    for copy in loads[5:]:
        copy.wait()
    pl.semaphore_wait(barrier, ni - 1 + cp + group - 1)

    for t in range(LOOPS):
        exchange(t, ni - 1, ni, disp, disp_got, disp_s, disp_r, 1)
        attention_send([2, 4, 6] if t == 0 else [1, 7])
        if t == 0:
            for copy in weight_copies():
                copy.start()
            for copy in weight_copies():
                copy.wait_recv()
        for step in PLAN:
            stages[step[0]](t, int(step[1:]))
        if t == 0:
            attention_send([3, 5])
            route_tables(1)
        else:
            attention_finish()
        for c, at in enumerate(spans):
            wait_bytes(back_got.at[t, at, :], back_r.at[t, c])
        routed = jnp.dot(combine_t[t], back_got[t], preferred_element_type=F32)
        comb[t, my_g] = (routed[0:64] + routed[64:128]).astype(BF16)
        for k in others:
            combine_copy(t, k).start()
        for k in others[::-1]:
            combine_copy(t, k).wait_recv()
        for x in range(nx):
            pair = comb[t, 2 * x].astype(F32) + comb[t, 2 * x + 1].astype(F32)
            for j in range(jb):
                at = slice(x * fx + j * LANES, x * fx + (j + 1) * LANES)
                hidden[:, at] = (mixed[:, at] + pair[8 * j : 8 * j + 8]).astype(BF16).astype(F32)
        if t + 1 < LOOPS:
            dispatch_tiles(t + 1)
    hid_out[...] = hidden[0:rows, :].astype(BF16)

    for copy in weight_copies():
        copy.wait_send()
    for t in range(LOOPS):
        exchange_sent(t, disp, disp_s)
        exchange_sent(t, back, back_s)
        for c in range(len(CHUNKS)):
            for k in range(1, nx):
                gather_copy(t, c, k).wait_send()
                reduce_copy(t, c, k).wait_send()
        for k in range(1, group):
            combine_copy(t, k).wait_send()


def body(
    ne, nx,
    hidden_in, draft_embeds, norm_gains, queries, latent_cache, lengths, route_ids, route_weights,
    w_gate, w_up, w_down,
):
    rows, width = hidden_in.shape
    topk = route_ids.shape[2]
    fx = width // nx
    jb = fx // LANES
    ni = ne // 2
    nn = 16 * ni
    nc = len(CHUNKS)
    most = max(CHUNKS)
    half = 2 * most
    group = 2 * nx
    sizes = (ne, nx, rows, jb, topk, float(queries.shape[3]) ** (-0.5))
    hbm = pl.BlockSpec(memory_space=pltpu.HBM)
    vmem = pl.BlockSpec(memory_space=pltpu.VMEM)
    dma = pltpu.SemaphoreType.DMA
    scratch = [
        pltpu.SMEM(lengths.shape, jnp.int32),
        pltpu.SMEM((rows, LOOPS, topk), jnp.int32),
        pltpu.SMEM((rows, LOOPS, topk), F32),
        pltpu.VMEM(hidden_in.shape, BF16),
        pltpu.VMEM((rows, LOOPS, width), BF16),
        pltpu.VMEM(norm_gains.shape, F32),
        pltpu.VMEM(queries.shape, BF16),
        pltpu.VMEM((rows, latent_cache.shape[2], LANES), BF16),
        pltpu.VMEM((width, 4 * LANES), BF16),
        pltpu.VMEM((2 * LANES, width), BF16),
        pltpu.VMEM((8, width), F32),
        pltpu.VMEM((LOOPS, 8, width), F32),
        pltpu.VMEM((8, width), F32),
        pltpu.VMEM((LANES, LANES), F32),
        pltpu.VMEM((LOOPS, nn, LANES), BF16),
        pltpu.VMEM((LOOPS, LANES, nn), BF16),
        pltpu.VMEM((nc, jb * half, 16 * most), BF16),
        pltpu.VMEM((nc, 16 * most, jb * half), BF16),
        pltpu.VMEM((LOOPS, nn, LANES), BF16),
        pltpu.VMEM((LOOPS, nn, LANES), BF16),
        pltpu.VMEM((LOOPS, nc, nx, half, fx), BF16),
        pltpu.VMEM((LOOPS, nc, nx, half, fx), BF16),
        pltpu.VMEM((LOOPS, nc, nx - 1, half, fx), BF16),
        pltpu.VMEM((jb * half, LANES), BF16),
        pltpu.VMEM((LOOPS, nn, LANES), BF16),
        pltpu.VMEM((LOOPS, nn, LANES), BF16),
        pltpu.VMEM((LOOPS, group, 64, LANES), BF16),
        pltpu.VMEM((group, 16 * rows, LATENT), BF16),
        pltpu.VMEM((group - 1, 16 * rows, LATENT), BF16),
        pltpu.VMEM((group, 16, LANES), F32),
        pltpu.VMEM((group - 1, 16, LANES), F32),
        dma((3,)), dma((8,)), dma((2,)), dma((2,)),
        dma((LOOPS,)), dma((LOOPS, nc)),
        dma((LOOPS, nc, nx - 1)), dma((LOOPS, nc, nx - 1)),
        dma((LOOPS, nc, nx - 1)), dma((LOOPS, nc, nx - 1)),
        dma((LOOPS,)), dma((LOOPS, nc)),
        dma((LOOPS, group - 1)), dma((LOOPS, group - 1)),
        dma((2, group - 1)), dma((2, group - 1)),
    ]
    heads_here = queries.shape[2] // group
    return tuple(
        pl.pallas_call(
            functools.partial(kernel, sizes),
            out_shape=(
                jax.ShapeDtypeStruct((LOOPS, rows, heads_here, LATENT), BF16),
                jax.ShapeDtypeStruct((rows, width), BF16),
            ),
            in_specs=[hbm] * 11,
            out_specs=(vmem, vmem),
            scratch_shapes=scratch,
            compiler_params=pltpu.CompilerParams(
                collective_id=0, has_side_effects=True, vmem_limit_bytes=60 * 1024 * 1024
            ),
            name="draft_steps",
        )(
            hidden_in, jnp.swapaxes(draft_embeds, 0, 1), norm_gains, queries,
            jnp.swapaxes(latent_cache, 1, 2), lengths, jnp.swapaxes(route_ids, 0, 1),
            jnp.swapaxes(route_weights, 0, 1), w_gate[0], w_up[0], w_down[0],
        )
    )


def solution(mesh):
    in_specs = (
        P("expert", None),
        P(None, "expert", None),
        P(),
        P(None, "expert", None, None),
        P("expert", ("context", "pipe"), None),
        P("expert"),
        P(None, "expert", None),
        P(None, "expert", None),
        P("expert", None, ("context", "pipe")),
        P("expert", None, ("context", "pipe")),
        P("expert", ("context", "pipe"), None),
    )
    out_specs = (P(None, "expert", ("context", "pipe"), None), P("expert", None))
    run = functools.partial(body, mesh.shape["expert"], mesh.shape["context"])
    return jax.shard_map(run, mesh=mesh, in_specs=in_specs, out_specs=out_specs, check_vma=False)
```

time: 119 us -> 94.8 us (0.80)
  Pallas kernels: 110 us -> 90.9 us
  local copies, waits for them, and re-layouts: 8.12 us -> 3 us
    pallas_call x1, Pallas kernels: 110 us -> 90.9 us  [body(): pl.pallas_call(functools.partial(kernel, sizes), out_shape=(jax.ShapeDtyp...]
    unnamed x20 -> x2, local copies, waits for them, and re-layouts: 8.12 us -> 3 us
where the time goes in v2:
time: 94.8 us; the launch traced here: 94.6 us
  Pallas kernels  90.9 us (96%)
  local copies, waits for them, and re-layouts  3 us (3%)
    pallas_call x1, Pallas kernels, body(): pl.pallas_call(functools.partial(kernel, sizes), out_shape=(jax.ShapeDtyp...  90.9 us
    unnamed x2, local copies, waits for them, and re-layouts  3 us

profile of v2, /device:TPU:1, one launch (start us, length us, event | category | flops | bytes accessed | tf_op | source)
XLA Modules:
  0.0 94.6 jit_solution(15392966581498665065)
XLA Ops:
  0.6 90.9 %draft_steps.1 = (bf16[2,7,8,512]{3,2,1,0:T(8,128)(2,1)}, bf16[7,3584]{1,0:T(8,128)(2,1)}) custom-call(bf16[7,3584]{1,0:T(8,128)(2,1)} %hid_in.1, bf16[7,2,3584]{2,1,0:T(2,128)(2,1)} %bitcast.11, f32[2,3584]{1,0:T(2,128)} %gains_in.1, bf16[2,7,64,576]{3,2,1,0:T(8,128)(2,1)} %q_in.1, bf16[7,576,128]{2,1,0:T(8,128)(2,1)} %bitcast.7, s32[7]{0:T(128)} %lengths_in.1, ...), custom_call_target="tpu_custom_call" | custom-call | tf_op jit(solution)/shard_map/draft_steps/pallas_call | solution.py:495
  91.6 1.6 %copy.15 = bf16[2,7,8,512]{3,2,1,0:T(8,128)(2,1)} copy(bf16[2,7,8,512]{3,2,1,0:T(8,128)(2,1)} %get-tuple-element.4) | data formatting | bytes 229376
  93.1 1.4 %copy.16 = bf16[7,3584]{1,0:T(8,128)(2,1)} copy(bf16[7,3584]{1,0:T(8,128)(2,1)} %get-tuple-element.5) | data formatting | bytes 100352

commit v3 on v2

--- a/solution.py
+++ b/solution.py
@@ -388,7 +388,7 @@
 
     for t in range(LOOPS):
         exchange(t, ni - 1, ni, disp, disp_got, disp_s, disp_r, 1)
-        attention_send([2, 4, 6] if t == 0 else [1, 7])
+        attention_send([4, 3, 5] if t == 0 else [2, 6, 7])
         if t == 0:
             for copy in weight_copies():
                 copy.start()
@@ -397,13 +397,25 @@
         for step in PLAN:
             stages[step[0]](t, int(step[1:]))
         if t == 0:
-            attention_send([3, 5])
+            attention_send([1])
             route_tables(1)
         else:
             attention_finish()
+            for copy in weight_copies():
+                copy.wait_send()
+            exchange_sent(0, back, back_s)
+            for u in range(LOOPS):
+                exchange_sent(u, disp, disp_s)
+                for c in range(len(CHUNKS)):
+                    for k in range(1, nx):
+                        gather_copy(u, c, k).wait_send()
+                        reduce_copy(u, c, k).wait_send()
+            for k in range(1, group):
+                combine_copy(0, k).wait_send()
+        routed = jnp.zeros((LANES, LANES), F32)
         for c, at in enumerate(spans):
             wait_bytes(back_got.at[t, at, :], back_r.at[t, c])
-        routed = jnp.dot(combine_t[t], back_got[t], preferred_element_type=F32)
+            routed += jnp.dot(combine_t[t, :, at], back_got[t, at, :], preferred_element_type=F32)
         comb[t, my_g] = (routed[0:64] + routed[64:128]).astype(BF16)
         for k in others:
             combine_copy(t, k).start()
@@ -418,17 +430,9 @@
             dispatch_tiles(t + 1)
     hid_out[...] = hidden[0:rows, :].astype(BF16)
 
-    for copy in weight_copies():
-        copy.wait_send()
-    for t in range(LOOPS):
-        exchange_sent(t, disp, disp_s)
-        exchange_sent(t, back, back_s)
-        for c in range(len(CHUNKS)):
-            for k in range(1, nx):
-                gather_copy(t, c, k).wait_send()
-                reduce_copy(t, c, k).wait_send()
-        for k in range(1, group):
-            combine_copy(t, k).wait_send()
+    exchange_sent(1, back, back_s)
+    for k in range(1, group):
+        combine_copy(1, k).wait_send()
 
 
 def body(

time: 94.8 us -> 94.6 us (level)
  no operation moved by 1% of the time
where the time goes in v3:
time: 94.6 us; the launch traced here: 94.5 us
  Pallas kernels  90.8 us (96%)
  local copies, waits for them, and re-layouts  3 us (3%)
    pallas_call x1, Pallas kernels, body(): pl.pallas_call(functools.partial(kernel, sizes), out_shape=(jax.ShapeDtyp...  90.8 us
    unnamed x2, local copies, waits for them, and re-layouts  3 us

profile of v3, /device:TPU:1, one launch (start us, length us, event | category | flops | bytes accessed | tf_op | source)
XLA Modules:
  0.0 94.5 jit_solution(17027670143914233877)
XLA Ops:
  0.6 90.8 %draft_steps.1 = (bf16[2,7,8,512]{3,2,1,0:T(8,128)(2,1)}, bf16[7,3584]{1,0:T(8,128)(2,1)}) custom-call(bf16[7,3584]{1,0:T(8,128)(2,1)} %hid_in.1, bf16[7,2,3584]{2,1,0:T(2,128)(2,1)} %bitcast.11, f32[2,3584]{1,0:T(2,128)} %gains_in.1, bf16[2,7,64,576]{3,2,1,0:T(8,128)(2,1)} %q_in.1, bf16[7,576,128]{2,1,0:T(8,128)(2,1)} %bitcast.7, s32[7]{0:T(128)} %lengths_in.1, ...), custom_call_target="tpu_custom_call" | custom-call | tf_op jit(solution)/shard_map/draft_steps/pallas_call | solution.py:499
  91.5 1.6 %copy.15 = bf16[2,7,8,512]{3,2,1,0:T(8,128)(2,1)} copy(bf16[2,7,8,512]{3,2,1,0:T(8,128)(2,1)} %get-tuple-element.4) | data formatting | bytes 229376
  93.0 1.4 %copy.16 = bf16[7,3584]{1,0:T(8,128)(2,1)} copy(bf16[7,3584]{1,0:T(8,128)(2,1)} %get-tuple-element.5) | data formatting | bytes 100352

commit v4 on v3

--- a/solution.py
+++ b/solution.py
@@ -419,12 +419,14 @@
         comb[t, my_g] = (routed[0:64] + routed[64:128]).astype(BF16)
         for k in others:
             combine_copy(t, k).start()
-        for k in others[::-1]:
-            combine_copy(t, k).wait_recv()
-        for x in range(nx):
+        for k in [0] + near_first:
+            for n in (2 * k, 2 * k + 1):
+                if n:
+                    combine_copy(t, n).wait_recv()
+            x = x_peer(nx - k) if k else cx
             pair = comb[t, 2 * x].astype(F32) + comb[t, 2 * x + 1].astype(F32)
             for j in range(jb):
-                at = slice(x * fx + j * LANES, x * fx + (j + 1) * LANES)
+                at = pl.ds(pl.multiple_of(x * fx + j * LANES, LANES), LANES)
                 hidden[:, at] = (mixed[:, at] + pair[8 * j : 8 * j + 8]).astype(BF16).astype(F32)
         if t + 1 < LOOPS:
             dispatch_tiles(t + 1)

time: 94.6 us -> 94.8 us (level)
  no operation moved by 1% of the time
where the time goes in v4:
time: 94.8 us; the launch traced here: 94.6 us
  Pallas kernels  90.9 us (96%)
  local copies, waits for them, and re-layouts  3 us (3%)
    pallas_call x1, Pallas kernels, body(): pl.pallas_call(functools.partial(kernel, sizes), out_shape=(jax.ShapeDtyp...  90.9 us
    unnamed x2, local copies, waits for them, and re-layouts  3 us

profile of v4, /device:TPU:1, one launch (start us, length us, event | category | flops | bytes accessed | tf_op | source)
XLA Modules:
  0.0 94.6 jit_solution(8953660722013218075)
XLA Ops:
  0.6 90.9 %draft_steps.1 = (bf16[2,7,8,512]{3,2,1,0:T(8,128)(2,1)}, bf16[7,3584]{1,0:T(8,128)(2,1)}) custom-call(bf16[7,3584]{1,0:T(8,128)(2,1)} %hid_in.1, bf16[7,2,3584]{2,1,0:T(2,128)(2,1)} %bitcast.11, f32[2,3584]{1,0:T(2,128)} %gains_in.1, bf16[2,7,64,576]{3,2,1,0:T(8,128)(2,1)} %q_in.1, bf16[7,576,128]{2,1,0:T(8,128)(2,1)} %bitcast.7, s32[7]{0:T(128)} %lengths_in.1, ...), custom_call_target="tpu_custom_call" | custom-call | tf_op jit(solution)/shard_map/draft_steps/pallas_call | solution.py:501
  91.6 1.6 %copy.15 = bf16[2,7,8,512]{3,2,1,0:T(8,128)(2,1)} copy(bf16[2,7,8,512]{3,2,1,0:T(8,128)(2,1)} %get-tuple-element.4) | data formatting | bytes 229376
  93.1 1.4 %copy.16 = bf16[7,3584]{1,0:T(8,128)(2,1)} copy(bf16[7,3584]{1,0:T(8,128)(2,1)} %get-tuple-element.5) | data formatting | bytes 100352
